TPU v7x, 32 devices: a whole 2x2x4 slice. The times are simulated.
32 devices in a mesh: vol: 16 (over z, y, x), path: 2 (over core).
Axes of the slice: x: 2, y: 2, z: 4, core: 2. Of those that a mesh axis runs over, the one named last changes fastest.
Arguments:
- factors: bfloat16 [16, 2048], P(None, 'path'), may hold values from -6 to 6
- payoff: float32 [4, 2048], P(None, 'path'), may hold values from -6 to 6
- terminal: float32 [16, 2048], P('vol', 'path'), may hold values from 0.5 to 4
- decisions: int32 [3, 16, 2048], P(None, 'vol', 'path'), may hold values 0 or 1
- level_range: int32 [4, 2], replicated, may hold values from 1 to 15, as said below
- w_in_master: float32 [16, 16, 1024], P('vol'), may hold values from -1.5 to 1.5
- w_mid_master: float32 [16, 1024, 1024], P('vol', 'path'), may hold values from -0.1875 to 0.1875
- vec_master: float32 [16, 3, 1024], P('vol'), may hold values from -0.6 to 0.6
- w_in_copy: bfloat16 [16, 16, 1024], P('vol'), may hold values from -1.5 to 1.5
- w_mid_copy: bfloat16 [16, 1024, 1024], P('vol', 'path'), may hold values from -0.1875 to 0.1875
- mom_in: float32 [16, 16, 1024], P('vol'), may hold values from -0.6 to 0.6
- mom_mid: float32 [16, 1024, 1024], P('vol', 'path'), may hold values from -0.6 to 0.6
- mom_vec: float32 [16, 3, 1024], P('vol'), may hold values from -0.6 to 0.6
Outputs:
- level_value: float32 [16], P('vol')
- new_w_in: float32 [16, 16, 1024], P('vol')
- new_w_mid: float32 [16, 1024, 1024], P('vol', 'path')
- new_vec: float32 [16, 3, 1024], P('vol')
- new_mom_in: float32 [16, 16, 1024], P('vol')
- new_mom_mid: float32 [16, 1024, 1024], P('vol', 'path')
- new_mom_vec: float32 [16, 3, 1024], P('vol')
- new_in_copy: bfloat16 [16, 16, 1024], P('vol')
- new_mid_copy: bfloat16 [16, 1024, 1024], P('vol', 'path')
Inputs may be any that keep to these rules, and one draw needn't show every extreme that they name: At every date level_range[s, 0] <= level_range[s, 1] and level 0 lies below the range; at dates 1 to 3 the range starts at level 1; at date 0 the range holds exactly 8 levels.
All inputs are finite; a program needn't handle non-finite values. No bound on the sum of `decisions` on one device may be relied on, other than what follows from the above.
Results may differ from a plain program's by a relative error of at most 0.015.
Values may be sent and summed in bfloat16 or wider, within the bound.
No kernel may reach another device: no remote copies, remote signals or barrier semaphores. Data moves between devices by JAX's collectives and lax.ppermute only.
A program may use at most 64 MiB of HBM per device.

v0:
```python
import jax
import jax.numpy as jnp
from jax import lax
from jax.experimental import pallas as pl
from jax.experimental.pallas import tpu as pltpu
from jax.sharding import PartitionSpec as P

MOMENTUM = 0.9
STEP_SIZE = 0.01
LOWER_LEVELS = 4
CORE_SHIFTS = ((4, 3), (2, 1))
SMALL_ROWS = 24
LANES = 128
VMEM_LIMIT = 30 * 1024 * 1024
F32, BF16 = jnp.float32, jnp.bfloat16
VMEM_SPEC = pl.BlockSpec(memory_space=pltpu.VMEM)
HBM_SPEC = pl.BlockSpec(memory_space=pltpu.HBM)


def far(value):
    return pltpu.with_memory_space_constraint(value, pltpu.HBM)


def shape(*dims, dtype=F32):
    return jax.ShapeDtypeStruct(dims, dtype)


def call(kernel, out_shape, in_specs, name, flops, out_specs=None, scratch=()):
    return pl.pallas_call(
        kernel,
        out_shape=out_shape,
        in_specs=in_specs,
        out_specs=out_specs or [VMEM_SPEC] * len(out_shape),
        scratch_shapes=list(scratch),
        compiler_params=pltpu.CompilerParams(vmem_limit_bytes=VMEM_LIMIT),
        cost_estimate=pl.CostEstimate(flops=flops, bytes_accessed=1 << 20, transcendentals=0),
        name=name,
    )


def half_columns(flip, half, width):
    return pl.ds(pl.multiple_of((flip ^ half) * width, width), width)


def is_active(flags):
    return flags[0, 0] > 0.5


def fetch(
    terminal, decisions, ranges, payoff, factors, w_in, vectors,
    rows, payoff_out, factors_out, w_in_out, vectors_out, flags,
    terminal_here, decisions_here, ranges_here, sems,
):
    copies = [
        pltpu.make_async_copy(source, target, sems.at[index])
        for index, (source, target) in enumerate(
            (
                (ranges, ranges_here),
                (terminal, terminal_here),
                (decisions, decisions_here),
                (payoff, payoff_out),
                (factors, factors_out),
                (w_in, w_in_out),
                (vectors, vectors_out),
            )
        )
    ]
    for copy in copies:
        copy.start()
    for copy in copies[:3]:
        copy.wait()
    level = lax.axis_index("vol")
    dates = payoff.shape[0]
    rows[0:1, :] = terminal_here[...]
    for date in range(dates):
        low, high = ranges_here[0, date], ranges_here[1, date]
        inside = jnp.where(jnp.logical_and(level >= low, level <= high), 1.0, 0.0)
        above = jnp.where(level > high, 1.0, 0.0)
        if date == 0:
            flags[0:1, :] = jnp.full((1, LANES), inside)
            flags[1:2, :] = jnp.full((1, LANES), above)
        else:
            rows[dates - date : dates - date + 1, :] = inside * decisions_here[date - 1].astype(F32) + above
    for copy in copies[3:]:
        copy.wait()


def silu_parts(half):
    bent = jnp.tanh(half)
    upper = 1.0 + bent
    act = half * upper
    return act, upper + act * (1.0 - bent)


def first_layer(flip_of, flags, rows, factors, w_in, vectors, rows_out, hidden_one, slope_one):
    rows_out[...] = rows[...]

    @pl.when(is_active(flags))
    def _():
        flip = flip_of()
        hidden = w_in.shape[1]
        width, paths, tile, rows = hidden // 2, factors.shape[1], 256, 16
        for half in range(2):
            columns = half_columns(flip, half, width)
            weights = (0.5 * w_in[:, columns].astype(F32)).astype(BF16)
            bias = 0.5 * vectors[0, :, columns]
            place = slice(half * width, (half + 1) * width)
            for start in range(0, paths, tile):
                pre = lax.dot_general(
                    factors[:, start : start + tile],
                    weights,
                    (((0,), (0,)), ((), ())),
                    preferred_element_type=F32,
                )
                for row in range(0, tile, rows):
                    half_pre = pre[row : row + rows] + bias
                    bent = jnp.tanh(half_pre)
                    squash = 0.5 + 0.5 * bent
                    half_act = half_pre * squash
                    here = slice(start + row, start + row + rows)
                    hidden_one[here, place] = half_act.astype(BF16)
                    slope_one[here, place] = squash + half_act * (1.0 - bent)


def continuation(level, payoff, row_sets):
    dates = payoff.shape[0]
    conts = [jnp.where(level >= below, rows[0:1, :], 0.0) for below, rows in enumerate(row_sets)]
    for date in range(dates - 1, 0, -1):
        updated = []
        for below in range(len(conts) - 1):
            taken = row_sets[below][dates - date : dates - date + 1, :]
            value = taken * (payoff[date : date + 1, :] + conts[below + 1]) + (1.0 - taken) * conts[below]
            updated.append(jnp.where(level >= below, value, 0.0))
        conts = updated
    return conts


def crossing_rows(first, second, after, out):
    del after
    start = 0
    for value in (first, second):
        count = value.shape[0] // 2
        out[start : start + count, :] = value[count:, :]
        start += count


def second_forward(flags, hidden_one, w_own, w_other, vectors, weighted, act_two, partial, joined):
    @pl.when(is_active(flags))
    def _():
        paths, hidden = hidden_one.shape
        width, rows = hidden // 2, 8
        bias, head = 0.5 * vectors[1], vectors[2]
        half_head = 0.5 * head
        joined[:width, :] = w_own[...]
        joined[width:, :] = w_other[...]
        pre = jnp.dot(hidden_one[...], joined[...], preferred_element_type=F32)
        for row in range(0, paths, rows):
            here = slice(row, row + rows)
            act, slope = silu_parts(pre[here] + bias)
            weighted[here, :] = slope * half_head
            act_two[here, :] = act
            terms = act * head
            part = terms[:, :LANES]
            for lane in range(LANES, hidden, LANES):
                part += terms[:, lane : lane + LANES]
            partial[here, :] = part


def exercise_chance(flags, partial, after, chance, parts):
    del after

    @pl.when(is_active(flags))
    def _():
        paths, rows = partial.shape[0], 16
        for row in range(0, paths, rows):
            here = slice(row, row + rows)
            part = partial[here, :]
            upper = part.astype(BF16)
            parts[here, :LANES] = upper
            parts[here, LANES:] = (part - upper.astype(F32)).astype(BF16)
        ones = jnp.ones((2 * LANES, LANES), BF16)
        logits = jnp.dot(parts[...], ones, preferred_element_type=F32)
        chance[...] = 0.5 + 0.5 * jnp.tanh(0.5 * logits)


def second_gradients(sets_of, flags, hidden_one, weighted, act_two, chances, payoff, *refs):
    *row_refs, d_two, grad_other, sums, gains = refs
    level = lax.axis_index("vol")
    paths, hidden = hidden_one.shape
    width, rows = hidden // 2, 16
    lane_tiles = hidden // LANES
    cont_here, cont_below = continuation(level, payoff, sets_of(row_refs))
    gain = payoff[0:1, :] + cont_below - cont_here
    base_value = flags[1, 0] * jnp.sum(gain) + jnp.sum(cont_here)

    @pl.when(jnp.logical_not(is_active(flags)))
    def _():
        grad_other[...] = jnp.zeros(grad_other.shape, BF16)
        sums[...] = jnp.zeros(sums.shape, F32)
        sums[2:3, :] = jnp.full((1, hidden), base_value, F32)

    @pl.when(is_active(flags))
    def _():
        gains[...] = jnp.transpose(jnp.broadcast_to(gain, (LANES, paths)))
        bias_sums = [jnp.zeros((8, LANES), F32) for _ in range(lane_tiles)]
        head_sums = [jnp.zeros((8, LANES), F32) for _ in range(lane_tiles)]
        value_sum = jnp.zeros((rows, LANES), F32)
        for row in range(0, paths, rows):
            here = slice(row, row + rows)
            chance = chances[here, :]
            weight = gains[here, :] * chance
            value_sum += weight
            d_logit = weight * (chance - 1.0)
            for lane in range(lane_tiles):
                place = slice(lane * LANES, (lane + 1) * LANES)
                d_pre = d_logit * weighted[here, place]
                scaled = d_logit * act_two[here, place]
                d_two[here, place] = d_pre.astype(BF16)
                for part in range(0, rows, 8):
                    bias_sums[lane] += d_pre[part : part + 8]
                    head_sums[lane] += scaled[part : part + 8]
        grad_other[...] = lax.dot_general(
            hidden_one[:, width:], d_two[...], (((0,), (0,)), ((), ())), preferred_element_type=F32
        ).astype(BF16)
        value_total = base_value + jnp.sum(value_sum) / LANES
        for lane in range(lane_tiles):
            place = slice(lane * LANES, (lane + 1) * LANES)
            sums[0:1, place] = jnp.sum(bias_sums[lane], axis=0, keepdims=True)
            sums[1:2, place] = jnp.sum(head_sums[lane], axis=0, keepdims=True)
        sums[2:3, :] = jnp.full((1, hidden), value_total, F32)
        sums[3:8, :] = jnp.zeros((5, hidden), F32)


def first_gradients(flip_of, flags, d_two, w_own, w_other, slope_one, factors, sums, small, d_one):
    count = factors.shape[0]
    hidden = d_two.shape[1]
    small[0 : count + 1, :] = jnp.zeros((count + 1, hidden), F32)
    small[count + 1 : count + 4, :] = sums[0:3, :]
    small[count + 4 : SMALL_ROWS, :] = jnp.zeros((SMALL_ROWS - count - 4, hidden), F32)

    @pl.when(is_active(flags))
    def _():
        flip = flip_of()
        paths = d_two.shape[0]
        width, tile, rows = hidden // 2, 512, 16
        for half, weights in enumerate((w_own, w_other)):
            place = slice(half * width, (half + 1) * width)
            bias_sum = jnp.zeros((8, width), F32)
            for start in range(0, paths, tile):
                d_hidden = lax.dot_general(
                    d_two[start : start + tile, :],
                    weights[...],
                    (((1,), (1,)), ((), ())),
                    preferred_element_type=F32,
                )
                for row in range(0, tile, rows):
                    here = slice(start + row, start + row + rows)
                    d_pre = d_hidden[row : row + rows] * slope_one[here, place]
                    d_one[here, place] = d_pre.astype(BF16)
                    for part in range(0, rows, 8):
                        bias_sum += d_pre[part : part + 8]
            columns = half_columns(flip, half, width)
            small[0:count, columns] = jnp.dot(factors[...], d_one[:, place], preferred_element_type=F32)
            small[count : count + 1, columns] = jnp.sum(bias_sum, axis=0, keepdims=True)


def own_gradient(hidden_one, d_two, columns):
    return lax.dot_general(
        hidden_one[:, columns], d_two[...], (((0,), (0,)), ((), ())), preferred_element_type=F32
    )


def plain_gradient(flags, hidden_one, d_two, grad_own):
    grad_own[...] = jnp.zeros(grad_own.shape, BF16)

    @pl.when(is_active(flags))
    def _():
        grad_own[...] = own_gradient(hidden_one, d_two, slice(0, grad_own.shape[0])).astype(BF16)


class Sends:
    def __init__(self, sems):
        self.sems, self.copies = sems, []

    def __call__(self, source, target):
        copy = pltpu.make_async_copy(source, target, self.sems.at[len(self.copies)])
        copy.start()
        self.copies.append(copy)

    def finish(self):
        for copy in self.copies:
            copy.wait()


def middle_update(block, paired, flags, *refs):
    if paired:
        hidden_one, d_two, *refs = refs
    grad, mom_mid, w_mid, new_mom, new_w, new_copy, mom_here, w_here, copy_here, sems = refs

    def write(gradient_of):
        sends = Sends(sems)
        for start in range(0, mom_mid.shape[0], block):
            here = pl.ds(start, block)
            momentum = MOMENTUM * mom_mid[here, :] + 2.0 * gradient_of(start, here)
            mom_here[here, :] = momentum
            master = w_mid[here, :] - STEP_SIZE * momentum
            w_here[here, :] = master
            copy_here[here, :] = master.astype(BF16)
            sends(mom_here.at[here], new_mom.at[here])
            sends(w_here.at[here], new_w.at[here])
            sends(copy_here.at[here], new_copy.at[here])
        sends.finish()

    if not paired:
        write(lambda start, here: grad[here, :].astype(F32))
        return

    @pl.when(is_active(flags))
    def _():
        write(
            lambda start, here: own_gradient(hidden_one, d_two, slice(start, start + block))
            + grad[here, :].astype(F32)
        )

    @pl.when(jnp.logical_not(is_active(flags)))
    def _():
        write(lambda start, here: grad[here, :].astype(F32))


def small_update(
    paths_total, after, small_own, small_other, mom_in, w_in, mom_vec, vec,
    value, new_w_in, new_vec, new_mom_in, new_mom_vec, new_copy,
    value_here, w_in_here, vec_here, mom_in_here, mom_vec_here, copy_here, sems,
):
    del after
    sends = Sends(sems)
    small = small_own[...] + small_other[...]
    count = mom_in.shape[0]
    mom_first = MOMENTUM * mom_in[...] + small[:count]
    first = w_in[...] - STEP_SIZE * mom_first
    mom_in_here[...] = mom_first
    w_in_here[...] = first
    copy_here[...] = first.astype(BF16)
    for row in range(3):
        mom_row = MOMENTUM * mom_vec[row] + small[count + row : count + row + 1]
        mom_vec_here[row] = mom_row
        vec_here[row] = vec[row] - STEP_SIZE * mom_row
    sends(mom_in_here, new_mom_in)
    sends(w_in_here, new_w_in)
    sends(copy_here, new_copy)
    sends(mom_vec_here, new_mom_vec)
    sends(vec_here, new_vec)
    value_here[0] = small[count + 3, 0] / paths_total
    sends(value_here, value)
    sends.finish()


def step_of(mesh):
    levels, cores = mesh.shape["vol"], mesh.shape["path"]
    paired = cores == 2

    def flip_of():
        return lax.axis_index("path") if paired else 0

    def swap(value):
        return lax.ppermute(value, "path", [(0, 1), (1, 0)])

    def shards(
        factors, payoff, terminal, decisions, level_range, w_in_master, w_mid_master, vec_master,
        w_in_copy, w_mid_copy, mom_in, mom_mid, mom_vec,
    ):
        dates, paths = payoff.shape
        count, hidden = w_in_copy.shape[1:]
        width = hidden // 2
        square = 2 * paths * hidden * hidden
        if paired:
            w_own = w_mid_copy[0]
            w_other = swap(w_own)
        else:
            w_full = lax.all_gather(w_mid_copy[0], "path", axis=0, tiled=True)
            w_own, w_other = w_full[:width], w_full[width:]
        vec_hbm = vec_master.transpose(1, 0, 2)
        rows, payoff_near, factors_near, w_in_near, vectors, flags = call(
            fetch,
            (
                shape(dates, paths),
                shape(dates, paths),
                shape(count, paths, dtype=BF16),
                shape(count, hidden, dtype=BF16),
                shape(3, 1, hidden),
                shape(8, LANES),
            ),
            [HBM_SPEC] * 7,
            "fetch",
            0,
            scratch=(
                pltpu.VMEM((1, paths), F32),
                pltpu.VMEM((dates - 1, 1, paths), jnp.int32),
                pltpu.SMEM((2, dates), jnp.int32),
                pltpu.SemaphoreType.DMA((7,)),
            ),
        )(*(far(value) for value in (terminal, decisions, level_range.T, payoff, factors, w_in_copy[0], vec_hbm)))

        rows_after, hidden_one, slope_one = call(
            lambda *refs: first_layer(flip_of, *refs),
            (shape(dates, paths), shape(paths, hidden, dtype=BF16), shape(paths, hidden)),
            [VMEM_SPEC] * 5,
            "first_layer",
            square,
        )(flags, rows, factors_near, w_in_near, vectors)
        if paired:
            both = jnp.concatenate([rows_after, swap(rows)])
            lower = [
                lax.ppermute(
                    both,
                    ("vol", "path"),
                    [
                        (here * 2 + core, (here + below[core]) % levels * 2 + core)
                        for here in range(levels)
                        for core in range(2)
                    ],
                )
                for below in CORE_SHIFTS
            ]
        else:
            row_arrays = (rows,) + tuple(
                lax.ppermute(rows, "vol", [(here, (here + below) % levels) for here in range(levels)])
                for below in range(1, LOWER_LEVELS + 1)
            )

        def sets_of(refs):
            if not paired:
                return [ref[...] for ref in refs]
            own, *lower, crossing = (ref[...] for ref in refs)
            even = lax.axis_index("path") == 0
            sets, start = {0: own}, 0
            for (low, high), value in zip(CORE_SHIFTS, lower):
                size = value.shape[0] // 2
                direct, crossed = value[:size], crossing[start : start + size]
                sets[low] = jnp.where(even, direct, crossed)
                sets[high] = jnp.where(even, crossed, direct)
                start += size
            return [sets[below] for below in range(LOWER_LEVELS + 1)]

        weighted, act_two, partial = call(
            second_forward,
            (shape(paths, hidden), shape(paths, hidden), shape(paths, LANES)),
            [VMEM_SPEC] * 5,
            "second_forward",
            square,
            scratch=(pltpu.VMEM((hidden, hidden), BF16),),
        )(flags, hidden_one, w_own, w_other, vectors)
        after = partial
        if paired:
            crossed = sum(value.shape[0] for value in lower) // 2
            (after,) = call(
                crossing_rows, (shape(crossed, paths),), [VMEM_SPEC] * 3, "crossing_rows", 0
            )(*lower, partial)
            row_arrays = (rows, *lower, swap(after))
        (chances,) = call(
            exercise_chance,
            (shape(paths, LANES),),
            [VMEM_SPEC] * 3,
            "exercise_chance",
            square,
            scratch=(pltpu.VMEM((paths, 2 * LANES), BF16),),
        )(flags, partial, after)
        d_two, grad_other, sums = call(
            lambda *refs: second_gradients(sets_of, *refs),
            (
                shape(paths, hidden, dtype=BF16),
                shape(width, hidden, dtype=BF16),
                shape(8, hidden),
            ),
            [VMEM_SPEC] * (6 + len(row_arrays)),
            "second_gradients",
            square,
            scratch=(pltpu.VMEM((paths, LANES), F32),),
        )(flags, hidden_one, weighted, act_two, chances, payoff_near, *row_arrays)
        if paired:
            grad_other = swap(grad_other)
        (small,) = call(
            lambda *refs: first_gradients(flip_of, *refs),
            (shape(SMALL_ROWS, hidden),),
            [VMEM_SPEC] * 7,
            "first_gradients",
            square,
            scratch=(pltpu.VMEM((paths, hidden), BF16),),
        )(flags, d_two, w_own, w_other, slope_one, factors_near, sums)
        if paired:
            small_other = swap(small)
            gradients = (hidden_one, d_two, grad_other)
        else:
            (grad_own,) = call(
                plain_gradient,
                (shape(width, hidden, dtype=BF16),),
                [VMEM_SPEC] * 3,
                "plain_gradient",
                square,
            )(flags, hidden_one, d_two)
            grads = jnp.concatenate([grad_own, grad_other])
            gradients = (lax.psum_scatter(grads, "path", scatter_dimension=0, tiled=True),)
            small = lax.psum(small, "path")
            small_other = jnp.zeros_like(small)
        own_rows = w_mid_copy.shape[1]
        block = min(128, own_rows)
        outs = (
            shape(own_rows, hidden),
            shape(own_rows, hidden),
            shape(own_rows, hidden, dtype=BF16),
        )
        new_mom_mid, new_w_mid, mid_copy = call(
            lambda *refs: middle_update(block, paired, *refs),
            outs,
            [VMEM_SPEC] * (3 + len(gradients)),
            "middle_update",
            square,
            out_specs=[HBM_SPEC] * 3,
            scratch=[pltpu.VMEM(out.shape, out.dtype) for out in outs]
            + [pltpu.SemaphoreType.DMA((3 * (own_rows // block),))],
        )(flags, *gradients, mom_mid[0], w_mid_master[0])
        outs = (
            shape(1),
            shape(count, hidden),
            shape(3, 1, hidden),
            shape(count, hidden),
            shape(3, 1, hidden),
            shape(count, hidden, dtype=BF16),
        )
        value, new_w_in, new_vec, new_mom_in, new_mom_vec, in_copy = call(
            lambda *refs: small_update(paths * cores, *refs),
            outs,
            [HBM_SPEC] + [VMEM_SPEC] * 6,
            "small_update",
            0,
            out_specs=[HBM_SPEC] * 6,
            scratch=[pltpu.SMEM((1,), F32)]
            + [pltpu.VMEM(out.shape, out.dtype) for out in outs[1:]]
            + [pltpu.SemaphoreType.DMA((6,))],
        )(far(new_mom_mid), small, small_other, mom_in[0], w_in_master[0], mom_vec.transpose(1, 0, 2), vectors)
        return (
            value,
            new_w_in[None],
            new_w_mid[None],
            new_vec.transpose(1, 0, 2),
            new_mom_in[None],
            new_mom_mid[None],
            new_mom_vec.transpose(1, 0, 2),
            in_copy[None],
            mid_copy[None],
        )

    return shards


def solution(mesh):
    vectors = P("vol", None, None)
    middle = P("vol", "path", None)
    in_specs = (
        P(None, "path"),
        P(None, "path"),
        P("vol", "path"),
        P(None, "vol", "path"),
        P(),
        vectors,
        middle,
        vectors,
        vectors,
        middle,
        vectors,
        middle,
        vectors,
    )
    out_specs = (P("vol"), vectors, middle, vectors, vectors, middle, vectors, vectors, middle)
    return jax.shard_map(step_of(mesh), mesh=mesh, in_specs=in_specs, out_specs=out_specs, check_vma=False)
```

profile of v0, /device:TPU:17, one launch (start us, length us, event | category | flops | bytes accessed | tf_op | source)
XLA Modules:
  0.0 21.2 jit_solution(10128037590546964790)
XLA Ops:
  0.6 0.7 %collective-permute-start = (bf16[512,1024]{1,0:T(8,128)(2,1)}, bf16[512,1024]{1,0:T(8,128)(2,1)S(1)}, u32[]{:S(2)}, u32[]{:S(2)}) collective-permute-start(bf16[512,1024]{1,0:T(8,128)(2,1)} %bitcast.19), channel_id=1, source_target_pairs={{0,1},{1,0},{2,3},{3,2},{4,5},{5,4},{6,7},{7,6},{8,9},{9,8},{10,11... | collective-permute-start | bytes 3145736 | tf_op jit(solution)/shard_map/ppermute | solution.py:366
  1.4 0.9 %fetch.1 = (f32[4,1024]{1,0:T(4,128)S(1)}, f32[4,1024]{1,0:T(4,128)S(1)}, bf16[16,1024]{1,0:T(8,128)(2,1)S(1)}, bf16[16,1024]{1,0:T(8,128)(2,1)S(1)}, f32[3,1,1024]{2,1,0:T(1,128)S(1)}, /*index=5*/f32[8,128]{1,0:T(8,128)S(1)}) custom-call(f32[1,1024]{1,0:T(1,128)} %terminal.1, s32[3,1,1024]{2,1,0:T(1,128)} %decisions.1, s32[2,4]{1,0:T(2,128)} %bitcast.28, ...), custom_call_target="tpu_custom_call" | custom-call | bytes 1048576 | tf_op jit(solution)/shard_map/fetch/pallas_call | solution.py:383
  2.3 0.1 collective-permute-start.1
  2.4 0.0 copy-start.2
  2.4 1.5 %first_layer.1 = (f32[4,1024]{1,0:T(4,128)S(1)}, bf16[1024,1024]{1,0:T(8,128)(2,1)S(1)}, f32[1024,1024]{1,0:T(8,128)S(1)}) custom-call(f32[8,128]{1,0:T(8,128)S(1)} %get-tuple-element.33.refs_0_.flags, f32[4,1024]{1,0:T(4,128)S(1)} %get-tuple-element.34.refs_1_.refs_6_, bf16[16,1024]{1,0:T(8,128)(2,1)S(1)} %get-tuple-element.35.refs_2_.refs_5_, ...), custom_call_target="tpu_custom_call" | custom-call | flops 2147483648 | bytes 1048576 | tf_op jit(solution)/shard_map/first_layer/pallas_call | solution.py:404
  3.8 0.0 collective-permute-done.1
  3.9 1.3 %collective-permute-start.3 = (f32[8,1024]{1,0:T(8,128)S(1)}, f32[8,1024]{1,0:T(8,128)S(1)}, u32[]{:S(2)}, u32[]{:S(2)}) collective-permute-start(f32[8,1024]{1,0:T(8,128)S(1)} %pad_maximum_fusion), channel_id=1, source_target_pairs={{0,4},{1,3},{2,6},{3,5},{4,8},{5,7},{6,10},{7,9},{8,12},{9,11},{10... | collective-permute-start | bytes 98312 | tf_op jit(solution)/shard_map/ppermute | solution.py:414
  5.1 2.2 %collective-permute-start.2 = (f32[8,1024]{1,0:T(8,128)S(1)}, f32[8,1024]{1,0:T(8,128)S(1)}, u32[]{:S(2)}, u32[]{:S(2)}) collective-permute-start(f32[8,1024]{1,0:T(8,128)S(1)} %pad_maximum_fusion), channel_id=1, source_target_pairs={{0,8},{1,7},{2,10},{3,9},{4,12},{5,11},{6,14},{7,13},{8,16},{9,15}... | collective-permute-start | bytes 98312 | tf_op jit(solution)/shard_map/ppermute | solution.py:414
  7.3 0.0 collective-permute-done.w_other.refs_3_
  7.3 0.0 copy-done.2
  7.3 3.0 %second_forward.1 = (f32[1024,1024]{1,0:T(8,128)S(1)}, f32[1024,1024]{1,0:T(8,128)S(1)}, f32[1024,128]{1,0:T(8,128)S(1)}) custom-call(f32[8,128]{1,0:T(8,128)S(1)} %get-tuple-element.33.refs_0_.flags, bf16[1024,1024]{1,0:T(8,128)(2,1)S(1)} %get-tuple-element.38.hidden_one.refs_1_, bf16[512,1024]{1,0:T(8,128)(2,1)S(1)} %bitcast.20, ...), custom_call_target="tpu_custom_call" | custom-call | flops 2147483648 | bytes 1048576 | tf_op jit(solution)/shard_map/second_forward/pallas_call | solution.py:445
  10.3 0.0 collective-permute-done.3.second.refs_8_
  10.3 0.0 collective-permute-done.2.first.refs_7_
  10.4 0.3 %collective-permute-start.4 = (f32[8,1024]{1,0:T(8,128)S(1)}, f32[8,1024]{1,0:T(8,128)S(1)}, u32[]{:S(2)}, u32[]{:S(2)}) collective-permute-start(f32[8,1024]{1,0:T(8,128)S(1)} %crossing_rows.1.after), channel_id=1, source_target_pairs={{0,1},{1,0},{2,3},{3,2},{4,5},{5,4},{6,7},{7,6},{8,9},{9,8},{10,11... | collective-permute-start | bytes 98312 | tf_op jit(solution)/shard_map/ppermute | solution.py:366
  10.6 0.4 %exercise_chance.1.refs_4_ = f32[1024,128]{1,0:T(8,128)S(1)} custom-call(f32[8,128]{1,0:T(8,128)S(1)} %get-tuple-element.33.refs_0_.flags, f32[1024,128]{1,0:T(8,128)S(1)} %get-tuple-element.41.after.partial, f32[8,1024]{1,0:T(8,128)S(1)} %crossing_rows.1.after), custom_call_target="tpu_custom_call" | custom-call | flops 2147483648 | bytes 1048576 | tf_op jit(solution)/shard_map/exercise_chance/pallas_call | solution.py:460
  11.0 0.6 %collective-permute-done.4.refs_9_ = f32[8,1024]{1,0:T(8,128)S(1)} collective-permute-done((f32[8,1024]{1,0:T(8,128)S(1)}, f32[8,1024]{1,0:T(8,128)S(1)}, u32[]{:S(2)}, u32[]{:S(2)}) %collective-permute-start.4) | collective-permute-done | bytes 32800 | tf_op jit(solution)/shard_map/ppermute | solution.py:366
  11.6 2.2 %second_gradients.1 = (bf16[1024,1024]{1,0:T(8,128)(2,1)S(1)}, bf16[512,1024]{1,0:T(8,128)(2,1)S(1)}, f32[8,1024]{1,0:T(8,128)S(1)}) custom-call(f32[8,128]{1,0:T(8,128)S(1)} %get-tuple-element.33.refs_0_.flags, bf16[1024,1024]{1,0:T(8,128)(2,1)S(1)} %get-tuple-element.38.hidden_one.refs_1_, f32[1024,1024]{1,0:T(8,128)S(1)} %get-tuple-element.39.refs_2_, ...), custom_call_target="tpu_custom_call" | custom-call | flops 2147483648 | bytes 1048576 | tf_op jit(solution)/shard_map/second_gradients/pallas_call | solution.py:468
  13.8 0.3 %collective-permute-start.5 = (bf16[512,1024]{1,0:T(8,128)(2,1)S(1)}, bf16[512,1024]{1,0:T(8,128)(2,1)S(1)}, u32[]{:S(2)}, u32[]{:S(2)}) collective-permute-start(bf16[512,1024]{1,0:T(8,128)(2,1)S(1)} %get-tuple-element.45), channel_id=1, source_target_pairs={{0,1},{1,0},{2,3},{3,2},{4,5},{5,4},{6,7},{7,6},{8,9},{9,8},{10,11... | collective-permute-start | bytes 3145736 | tf_op jit(solution)/shard_map/ppermute | solution.py:366
  14.1 2.8 %first_gradients.1.refs_1_ = f32[24,1024]{1,0:T(8,128)S(1)} custom-call(f32[8,128]{1,0:T(8,128)S(1)} %get-tuple-element.33.refs_0_.flags, bf16[1024,1024]{1,0:T(8,128)(2,1)S(1)} %get-tuple-element.44.refs_2_.refs_1_, bf16[512,1024]{1,0:T(8,128)(2,1)S(1)} %bitcast.21, bf16[512,1024]{1,0:T(8,128)(2,1)S(1)} %collective-permute-done.w_other.refs_3_, ...), custom_call_target="tpu_custom_call" | custom-call | flops 2147483648 | bytes 1048576 | tf_op jit(solution)/shard_map/first_gradients/pallas_call | solution.py:482
  16.9 0.3 %collective-permute-start.6 = (f32[24,1024]{1,0:T(8,128)S(1)}, f32[24,1024]{1,0:T(8,128)S(1)}, u32[]{:S(2)}, u32[]{:S(2)}) collective-permute-start(f32[24,1024]{1,0:T(8,128)S(1)} %first_gradients.1.refs_1_), channel_id=1, source_target_pairs={{0,1},{1,0},{2,3},{3,2},{4,5},{5,4},{6,7},{7,6},{8,9},{9,8},{10,11... | collective-permute-start | bytes 294920 | tf_op jit(solution)/shard_map/ppermute | solution.py:366
  17.2 0.0 collective-permute-done.5.refs_3_
  17.2 0.0 copy-done
  17.2 0.0 copy-done.1
  17.2 0.0 copy-start.3
  17.2 0.0 copy-start.4
  17.2 0.0 copy-start.5
  17.2 3.2 %middle_update.1 = (f32[512,1024]{1,0:T(8,128)}, f32[512,1024]{1,0:T(8,128)}, bf16[512,1024]{1,0:T(8,128)(2,1)}) custom-call(f32[8,128]{1,0:T(8,128)S(1)} %get-tuple-element.33.refs_0_.flags, bf16[1024,1024]{1,0:T(8,128)(2,1)S(1)} %get-tuple-element.38.hidden_one.refs_1_, bf16[1024,1024]{1,0:T(8,128)(2,1)S(1)} %get-tuple-element.44.refs_2_.refs_1_, ...), custom_call_target="tpu_custom_call" | custom-call | flops 2147483648 | bytes 1048576 | tf_op jit(solution)/shard_map/middle_update/pallas_call | solution.py:512
  20.5 0.0 collective-permute-done.6.refs_2_
  20.5 0.0 copy-done.3
  20.5 0.0 copy-done.4
  20.5 0.0 copy-done.5
  20.5 0.7 %small_update.1 = (f32[1]{0:T(128)}, f32[16,1024]{1,0:T(8,128)}, f32[3,1,1024]{2,1,0:T(1,128)}, f32[16,1024]{1,0:T(8,128)}, f32[3,1,1024]{2,1,0:T(1,128)}, /*index=5*/bf16[16,1024]{1,0:T(8,128)(2,1)}) custom-call(f32[512,1024]{1,0:T(8,128)} %get-tuple-element.46.refs_0_, f32[24,1024]{1,0:T(8,128)S(1)} %first_gradients.1.refs_1_, ...), custom_call_target="tpu_custom_call" | custom-call | bytes 1048576 | tf_op jit(solution)/shard_map/small_update/pallas_call | solution.py:530
  (4 shorter events, 0.0 us)
Async XLA Ops:
  0.6 6.7 %collective-permute-start = (bf16[512,1024]{1,0:T(8,128)(2,1)}, bf16[512,1024]{1,0:T(8,128)(2,1)S(1)}, u32[]{:S(2)}, u32[]{:S(2)}) collective-permute-start(bf16[512,1024]{1,0:T(8,128)(2,1)} %bitcast.19), channel_id=1, source_target_pairs={{0,1},{1,0},{2,3},{3,2},{4,5},{5,4},{6,7},{7,6},{8,9},{9,8},{10,11... | collective-permute-start | bytes 3145736 | tf_op jit(solution)/shard_map/ppermute | solution.py:366
  2.3 1.6 %collective-permute-start.1 = (f32[4,1024]{1,0:T(4,128)S(1)}, f32[4,1024]{1,0:T(4,128)S(1)}, u32[]{:S(2)}, u32[]{:S(2)}) collective-permute-start(f32[4,1024]{1,0:T(4,128)S(1)} %get-tuple-element.34.refs_1_.refs_6_), channel_id=1, source_target_pairs={{0,1},{1,0},{2,3},{3,2},{4,5},{5,4},{6,7},{7,6},{8,9},{9,8},{10,11... | collective-permute-start | bytes 49160 | tf_op jit(solution)/shard_map/ppermute | solution.py:366
  2.4 4.9 %copy-start.2 = (bf16[1,512,1024]{2,1,0:T(8,128)(2,1)S(1)}, bf16[1,512,1024]{2,1,0:T(8,128)(2,1)}, u32[]{:S(2)}) copy-start(bf16[1,512,1024]{2,1,0:T(8,128)(2,1)} %param.22) | copy-start | bytes 3145732
  3.9 6.5 %collective-permute-start.3 = (f32[8,1024]{1,0:T(8,128)S(1)}, f32[8,1024]{1,0:T(8,128)S(1)}, u32[]{:S(2)}, u32[]{:S(2)}) collective-permute-start(f32[8,1024]{1,0:T(8,128)S(1)} %pad_maximum_fusion), channel_id=1, source_target_pairs={{0,4},{1,3},{2,6},{3,5},{4,8},{5,7},{6,10},{7,9},{8,12},{9,11},{10... | collective-permute-start | bytes 98312 | tf_op jit(solution)/shard_map/ppermute | solution.py:414
  5.1 5.2 %collective-permute-start.2 = (f32[8,1024]{1,0:T(8,128)S(1)}, f32[8,1024]{1,0:T(8,128)S(1)}, u32[]{:S(2)}, u32[]{:S(2)}) collective-permute-start(f32[8,1024]{1,0:T(8,128)S(1)} %pad_maximum_fusion), channel_id=1, source_target_pairs={{0,8},{1,7},{2,10},{3,9},{4,12},{5,11},{6,14},{7,13},{8,16},{9,15}... | collective-permute-start | bytes 98312 | tf_op jit(solution)/shard_map/ppermute | solution.py:414
  10.4 1.3 %collective-permute-start.4 = (f32[8,1024]{1,0:T(8,128)S(1)}, f32[8,1024]{1,0:T(8,128)S(1)}, u32[]{:S(2)}, u32[]{:S(2)}) collective-permute-start(f32[8,1024]{1,0:T(8,128)S(1)} %crossing_rows.1.after), channel_id=1, source_target_pairs={{0,1},{1,0},{2,3},{3,2},{4,5},{5,4},{6,7},{7,6},{8,9},{9,8},{10,11... | collective-permute-start | bytes 98312 | tf_op jit(solution)/shard_map/ppermute | solution.py:366
  13.8 3.4 %collective-permute-start.5 = (bf16[512,1024]{1,0:T(8,128)(2,1)S(1)}, bf16[512,1024]{1,0:T(8,128)(2,1)S(1)}, u32[]{:S(2)}, u32[]{:S(2)}) collective-permute-start(bf16[512,1024]{1,0:T(8,128)(2,1)S(1)} %get-tuple-element.45), channel_id=1, source_target_pairs={{0,1},{1,0},{2,3},{3,2},{4,5},{5,4},{6,7},{7,6},{8,9},{9,8},{10,11... | collective-permute-start | bytes 3145736 | tf_op jit(solution)/shard_map/ppermute | solution.py:366
  14.1 3.1 %copy-start = (f32[1,512,1024]{2,1,0:T(8,128)S(1)}, f32[1,512,1024]{2,1,0:T(8,128)}, u32[]{:S(2)}) copy-start(f32[1,512,1024]{2,1,0:T(8,128)} %param.24) | copy-start | bytes 6291460
  14.1 3.1 %copy-start.1 = (f32[1,512,1024]{2,1,0:T(8,128)S(1)}, f32[1,512,1024]{2,1,0:T(8,128)}, u32[]{:S(2)}) copy-start(f32[1,512,1024]{2,1,0:T(8,128)} %param.19) | copy-start | bytes 6291460
  16.9 3.6 %collective-permute-start.6 = (f32[24,1024]{1,0:T(8,128)S(1)}, f32[24,1024]{1,0:T(8,128)S(1)}, u32[]{:S(2)}, u32[]{:S(2)}) collective-permute-start(f32[24,1024]{1,0:T(8,128)S(1)} %first_gradients.1.refs_1_), channel_id=1, source_target_pairs={{0,1},{1,0},{2,3},{3,2},{4,5},{5,4},{6,7},{7,6},{8,9},{9,8},{10,11... | collective-permute-start | bytes 294920 | tf_op jit(solution)/shard_map/ppermute | solution.py:366
  17.2 3.3 %copy-start.3 = (f32[1,16,1024]{2,1,0:T(8,128)S(1)}, f32[1,16,1024]{2,1,0:T(8,128)}, u32[]{:S(2)}) copy-start(f32[1,16,1024]{2,1,0:T(8,128)} %param.23) | copy-start | bytes 196612
  17.2 3.3 %copy-start.4 = (f32[1,16,1024]{2,1,0:T(8,128)S(1)}, f32[1,16,1024]{2,1,0:T(8,128)}, u32[]{:S(2)}) copy-start(f32[1,16,1024]{2,1,0:T(8,128)} %param.18) | copy-start | bytes 196612
  17.2 3.3 %copy-start.5 = (f32[1,3,1024]{2,0,1:T(1,128)S(1)}, f32[1,3,1024]{2,0,1:T(1,128)}, u32[]{:S(2)}) copy-start(f32[1,3,1024]{2,0,1:T(1,128)} %param.25) | copy-start | bytes 36868
where the time goes:
time: 21.5 us; the launch traced here: 21.2 us
  Pallas kernels  14.6 us (68%)
  starting transfers between devices  5.1 us (24%)
  between operations  0.8 us (4%)
  waiting for transfers between devices  0.66 us (3%)
    ppermute x2, starting transfers between devices, shards(): lax.ppermute(both, ('vol', 'path'), [(here * 2 + core, (here + below[core...  3.43 us
    pallas_call x1, Pallas kernels, shards(): call(lambda *refs: middle_update(block, paired, *refs), outs, [VMEM_SPEC]...  3.21 us
    pallas_call x1, Pallas kernels, shards(): call(second_forward, (shape(paths, hidden), shape(paths, hidden), shape(p...  3.02 us
    pallas_call x1, Pallas kernels, shards(): call(lambda *refs: first_gradients(flip_of, *refs), (shape(SMALL_ROWS, hi...  2.78 us
    pallas_call x1, Pallas kernels, shards(): call(lambda *refs: second_gradients(sets_of, *refs), (shape(paths, hidden...  2.18 us
    ppermute x5, starting transfers between devices, swap(): return lax.ppermute(value, 'path', [(0, 1), (1, 0)])  1.67 us
    pallas_call x1, Pallas kernels, shards(): call(lambda *refs: first_layer(flip_of, *refs), (shape(dates, paths), sha...  1.46 us
    pallas_call x1, Pallas kernels, shards(): call(fetch, (shape(dates, paths), shape(dates, paths), shape(count, paths...  0.89 us
  transfers between devices with their start and end apart: 7, of which 1 were waited for; matrix products, arithmetic and copies ran while one was open for 0% of the time, Pallas kernels for 55%

commit v1 on v0

--- a/solution.py
+++ b/solution.py
@@ -8,7 +8,7 @@
 MOMENTUM = 0.9
 STEP_SIZE = 0.01
 LOWER_LEVELS = 4
-CORE_SHIFTS = ((4, 3), (2, 1))
+CORE_SHIFTS = ((4, 2), (1, 3))
 SMALL_ROWS = 24
 LANES = 128
 VMEM_LIMIT = 30 * 1024 * 1024

time: 21.5 us -> 22.4 us (1.042)
  the two profiles are of different devices: /device:TPU:17 before, /device:TPU:7 now
where the time goes in v1:
time: 22.4 us; the launch traced here: 22.1 us
  Pallas kernels  14.6 us (65%)
  starting transfers between devices  6.14 us (27%)
  between operations  0.8 us (4%)
  waiting for transfers between devices  0.52 us (2%)
    ppermute x5, starting transfers between devices, swap(): return lax.ppermute(value, 'path', [(0, 1), (1, 0)])  3.58 us
    pallas_call x1, Pallas kernels, shards(): call(lambda *refs: middle_update(block, paired, *refs), outs, [VMEM_SPEC]...  3.21 us
    pallas_call x1, Pallas kernels, shards(): call(second_forward, (shape(paths, hidden), shape(paths, hidden), shape(p...  3.02 us
    pallas_call x1, Pallas kernels, shards(): call(lambda *refs: first_gradients(flip_of, *refs), (shape(SMALL_ROWS, hi...  2.78 us
    ppermute x2, starting transfers between devices, shards(): lax.ppermute(both, ('vol', 'path'), [(here * 2 + core, (here + below[core...  2.57 us
    pallas_call x1, Pallas kernels, shards(): call(lambda *refs: second_gradients(sets_of, *refs), (shape(paths, hidden...  2.18 us
    pallas_call x1, Pallas kernels, shards(): call(lambda *refs: first_layer(flip_of, *refs), (shape(dates, paths), sha...  1.45 us
    pallas_call x1, Pallas kernels, shards(): call(fetch, (shape(dates, paths), shape(dates, paths), shape(count, paths...  0.89 us
  transfers between devices with their start and end apart: 7, of which 1 were waited for; matrix products, arithmetic and copies ran while one was open for 0% of the time, Pallas kernels for 53%

profile of v1, /device:TPU:7, one launch (start us, length us, event | category | flops | bytes accessed | tf_op | source)
XLA Modules:
  0.0 22.1 jit_solution(13898102032611546309)
XLA Ops:
  0.6 0.7 %collective-permute-start = (bf16[512,1024]{1,0:T(8,128)(2,1)}, bf16[512,1024]{1,0:T(8,128)(2,1)S(1)}, u32[]{:S(2)}, u32[]{:S(2)}) collective-permute-start(bf16[512,1024]{1,0:T(8,128)(2,1)} %bitcast.19), channel_id=1, source_target_pairs={{0,1},{1,0},{2,3},{3,2},{4,5},{5,4},{6,7},{7,6},{8,9},{9,8},{10,11... | collective-permute-start | bytes 3145736 | tf_op jit(solution)/shard_map/ppermute | solution.py:366
  1.4 0.9 %fetch.1 = (f32[4,1024]{1,0:T(4,128)S(1)}, f32[4,1024]{1,0:T(4,128)S(1)}, bf16[16,1024]{1,0:T(8,128)(2,1)S(1)}, bf16[16,1024]{1,0:T(8,128)(2,1)S(1)}, f32[3,1,1024]{2,1,0:T(1,128)S(1)}, /*index=5*/f32[8,128]{1,0:T(8,128)S(1)}) custom-call(f32[1,1024]{1,0:T(1,128)} %terminal.1, s32[3,1,1024]{2,1,0:T(1,128)} %decisions.1, s32[2,4]{1,0:T(2,128)} %bitcast.28, ...), custom_call_target="tpu_custom_call" | custom-call | bytes 1048576 | tf_op jit(solution)/shard_map/fetch/pallas_call | solution.py:383
  2.3 0.1 collective-permute-start.1
  2.4 0.0 copy-start.2
  2.4 1.5 %first_layer.1 = (f32[4,1024]{1,0:T(4,128)S(1)}, bf16[1024,1024]{1,0:T(8,128)(2,1)S(1)}, f32[1024,1024]{1,0:T(8,128)S(1)}) custom-call(f32[8,128]{1,0:T(8,128)S(1)} %get-tuple-element.33.refs_0_.flags, f32[4,1024]{1,0:T(4,128)S(1)} %get-tuple-element.34.refs_1_.refs_6_, bf16[16,1024]{1,0:T(8,128)(2,1)S(1)} %get-tuple-element.35.refs_2_.refs_5_, ...), custom_call_target="tpu_custom_call" | custom-call | flops 2147483648 | bytes 1048576 | tf_op jit(solution)/shard_map/first_layer/pallas_call | solution.py:404
  3.8 0.0 collective-permute-done.1
  3.9 1.3 %collective-permute-start.3 = (f32[8,1024]{1,0:T(8,128)S(1)}, f32[8,1024]{1,0:T(8,128)S(1)}, u32[]{:S(2)}, u32[]{:S(2)}) collective-permute-start(f32[8,1024]{1,0:T(8,128)S(1)} %pad_maximum_fusion), channel_id=1, source_target_pairs={{0,2},{1,7},{2,4},{3,9},{4,6},{5,11},{6,8},{7,13},{8,10},{9,15},{1... | collective-permute-start | bytes 98312 | tf_op jit(solution)/shard_map/ppermute | solution.py:414
  5.2 1.2 %collective-permute-start.2 = (f32[8,1024]{1,0:T(8,128)S(1)}, f32[8,1024]{1,0:T(8,128)S(1)}, u32[]{:S(2)}, u32[]{:S(2)}) collective-permute-start(f32[8,1024]{1,0:T(8,128)S(1)} %pad_maximum_fusion), channel_id=1, source_target_pairs={{0,8},{1,5},{2,10},{3,7},{4,12},{5,9},{6,14},{7,11},{8,16},{9,13},... | collective-permute-start | bytes 98312 | tf_op jit(solution)/shard_map/ppermute | solution.py:414
  6.4 0.0 collective-permute-done.w_other.refs_3_
  6.4 0.0 copy-done.2
  6.4 3.0 %second_forward.1 = (f32[1024,1024]{1,0:T(8,128)S(1)}, f32[1024,1024]{1,0:T(8,128)S(1)}, f32[1024,128]{1,0:T(8,128)S(1)}) custom-call(f32[8,128]{1,0:T(8,128)S(1)} %get-tuple-element.33.refs_0_.flags, bf16[1024,1024]{1,0:T(8,128)(2,1)S(1)} %get-tuple-element.38.hidden_one.refs_1_, bf16[512,1024]{1,0:T(8,128)(2,1)S(1)} %bitcast.20, ...), custom_call_target="tpu_custom_call" | custom-call | flops 2147483648 | bytes 1048576 | tf_op jit(solution)/shard_map/second_forward/pallas_call | solution.py:445
  9.5 0.0 collective-permute-done.3.second.refs_8_
  9.5 0.0 collective-permute-done.2.first.refs_7_
  9.5 2.2 %collective-permute-start.4 = (f32[8,1024]{1,0:T(8,128)S(1)}, f32[8,1024]{1,0:T(8,128)S(1)}, u32[]{:S(2)}, u32[]{:S(2)}) collective-permute-start(f32[8,1024]{1,0:T(8,128)S(1)} %crossing_rows.1.after), channel_id=1, source_target_pairs={{0,1},{1,0},{2,3},{3,2},{4,5},{5,4},{6,7},{7,6},{8,9},{9,8},{10,11... | collective-permute-start | bytes 98312 | tf_op jit(solution)/shard_map/ppermute | solution.py:366
  11.7 0.4 %exercise_chance.1.refs_4_ = f32[1024,128]{1,0:T(8,128)S(1)} custom-call(f32[8,128]{1,0:T(8,128)S(1)} %get-tuple-element.33.refs_0_.flags, f32[1024,128]{1,0:T(8,128)S(1)} %get-tuple-element.41.after.partial, f32[8,1024]{1,0:T(8,128)S(1)} %crossing_rows.1.after), custom_call_target="tpu_custom_call" | custom-call | flops 2147483648 | bytes 1048576 | tf_op jit(solution)/shard_map/exercise_chance/pallas_call | solution.py:460
  12.0 0.5 %collective-permute-done.4.refs_9_ = f32[8,1024]{1,0:T(8,128)S(1)} collective-permute-done((f32[8,1024]{1,0:T(8,128)S(1)}, f32[8,1024]{1,0:T(8,128)S(1)}, u32[]{:S(2)}, u32[]{:S(2)}) %collective-permute-start.4) | collective-permute-done | bytes 32800 | tf_op jit(solution)/shard_map/ppermute | solution.py:366
  12.5 2.2 %second_gradients.1 = (bf16[1024,1024]{1,0:T(8,128)(2,1)S(1)}, bf16[512,1024]{1,0:T(8,128)(2,1)S(1)}, f32[8,1024]{1,0:T(8,128)S(1)}) custom-call(f32[8,128]{1,0:T(8,128)S(1)} %get-tuple-element.33.refs_0_.flags, bf16[1024,1024]{1,0:T(8,128)(2,1)S(1)} %get-tuple-element.38.hidden_one.refs_1_, f32[1024,1024]{1,0:T(8,128)S(1)} %get-tuple-element.39.refs_2_, ...), custom_call_target="tpu_custom_call" | custom-call | flops 2147483648 | bytes 1048576 | tf_op jit(solution)/shard_map/second_gradients/pallas_call | solution.py:468
  14.7 0.4 %collective-permute-start.5 = (bf16[512,1024]{1,0:T(8,128)(2,1)S(1)}, bf16[512,1024]{1,0:T(8,128)(2,1)S(1)}, u32[]{:S(2)}, u32[]{:S(2)}) collective-permute-start(bf16[512,1024]{1,0:T(8,128)(2,1)S(1)} %get-tuple-element.45), channel_id=1, source_target_pairs={{0,1},{1,0},{2,3},{3,2},{4,5},{5,4},{6,7},{7,6},{8,9},{9,8},{10,11... | collective-permute-start | bytes 3145736 | tf_op jit(solution)/shard_map/ppermute | solution.py:366
  15.1 2.8 %first_gradients.1.refs_1_ = f32[24,1024]{1,0:T(8,128)S(1)} custom-call(f32[8,128]{1,0:T(8,128)S(1)} %get-tuple-element.33.refs_0_.flags, bf16[1024,1024]{1,0:T(8,128)(2,1)S(1)} %get-tuple-element.44.refs_2_.refs_1_, bf16[512,1024]{1,0:T(8,128)(2,1)S(1)} %bitcast.21, bf16[512,1024]{1,0:T(8,128)(2,1)S(1)} %collective-permute-done.w_other.refs_3_, ...), custom_call_target="tpu_custom_call" | custom-call | flops 2147483648 | bytes 1048576 | tf_op jit(solution)/shard_map/first_gradients/pallas_call | solution.py:482
  17.9 0.2 collective-permute-start.6
  18.1 0.0 collective-permute-done.5.refs_3_
  18.1 0.0 copy-done
  18.1 0.0 copy-done.1
  18.1 0.0 copy-start.3
  18.1 0.0 copy-start.4
  18.1 0.0 copy-start.5
  18.1 3.2 %middle_update.1 = (f32[512,1024]{1,0:T(8,128)}, f32[512,1024]{1,0:T(8,128)}, bf16[512,1024]{1,0:T(8,128)(2,1)}) custom-call(f32[8,128]{1,0:T(8,128)S(1)} %get-tuple-element.33.refs_0_.flags, bf16[1024,1024]{1,0:T(8,128)(2,1)S(1)} %get-tuple-element.38.hidden_one.refs_1_, bf16[1024,1024]{1,0:T(8,128)(2,1)S(1)} %get-tuple-element.44.refs_2_.refs_1_, ...), custom_call_target="tpu_custom_call" | custom-call | flops 2147483648 | bytes 1048576 | tf_op jit(solution)/shard_map/middle_update/pallas_call | solution.py:512
  21.4 0.0 collective-permute-done.6.refs_2_
  21.4 0.0 copy-done.3
  21.4 0.0 copy-done.4
  21.4 0.0 copy-done.5
  21.4 0.7 %small_update.1 = (f32[1]{0:T(128)}, f32[16,1024]{1,0:T(8,128)}, f32[3,1,1024]{2,1,0:T(1,128)}, f32[16,1024]{1,0:T(8,128)}, f32[3,1,1024]{2,1,0:T(1,128)}, /*index=5*/bf16[16,1024]{1,0:T(8,128)(2,1)}) custom-call(f32[512,1024]{1,0:T(8,128)} %get-tuple-element.46.refs_0_, f32[24,1024]{1,0:T(8,128)S(1)} %first_gradients.1.refs_1_, ...), custom_call_target="tpu_custom_call" | custom-call | bytes 1048576 | tf_op jit(solution)/shard_map/small_update/pallas_call | solution.py:530
  (4 shorter events, 0.0 us)
Async XLA Ops:
  0.6 5.8 %collective-permute-start = (bf16[512,1024]{1,0:T(8,128)(2,1)}, bf16[512,1024]{1,0:T(8,128)(2,1)S(1)}, u32[]{:S(2)}, u32[]{:S(2)}) collective-permute-start(bf16[512,1024]{1,0:T(8,128)(2,1)} %bitcast.19), channel_id=1, source_target_pairs={{0,1},{1,0},{2,3},{3,2},{4,5},{5,4},{6,7},{7,6},{8,9},{9,8},{10,11... | collective-permute-start | bytes 3145736 | tf_op jit(solution)/shard_map/ppermute | solution.py:366
  2.3 1.6 %collective-permute-start.1 = (f32[4,1024]{1,0:T(4,128)S(1)}, f32[4,1024]{1,0:T(4,128)S(1)}, u32[]{:S(2)}, u32[]{:S(2)}) collective-permute-start(f32[4,1024]{1,0:T(4,128)S(1)} %get-tuple-element.34.refs_1_.refs_6_), channel_id=1, source_target_pairs={{0,1},{1,0},{2,3},{3,2},{4,5},{5,4},{6,7},{7,6},{8,9},{9,8},{10,11... | collective-permute-start | bytes 49160 | tf_op jit(solution)/shard_map/ppermute | solution.py:366
  2.4 4.1 %copy-start.2 = (bf16[1,512,1024]{2,1,0:T(8,128)(2,1)S(1)}, bf16[1,512,1024]{2,1,0:T(8,128)(2,1)}, u32[]{:S(2)}) copy-start(bf16[1,512,1024]{2,1,0:T(8,128)(2,1)} %param.22) | copy-start | bytes 3145732
  3.9 5.6 %collective-permute-start.3 = (f32[8,1024]{1,0:T(8,128)S(1)}, f32[8,1024]{1,0:T(8,128)S(1)}, u32[]{:S(2)}, u32[]{:S(2)}) collective-permute-start(f32[8,1024]{1,0:T(8,128)S(1)} %pad_maximum_fusion), channel_id=1, source_target_pairs={{0,2},{1,7},{2,4},{3,9},{4,6},{5,11},{6,8},{7,13},{8,10},{9,15},{1... | collective-permute-start | bytes 98312 | tf_op jit(solution)/shard_map/ppermute | solution.py:414
  5.2 4.3 %collective-permute-start.2 = (f32[8,1024]{1,0:T(8,128)S(1)}, f32[8,1024]{1,0:T(8,128)S(1)}, u32[]{:S(2)}, u32[]{:S(2)}) collective-permute-start(f32[8,1024]{1,0:T(8,128)S(1)} %pad_maximum_fusion), channel_id=1, source_target_pairs={{0,8},{1,5},{2,10},{3,7},{4,12},{5,9},{6,14},{7,11},{8,16},{9,13},... | collective-permute-start | bytes 98312 | tf_op jit(solution)/shard_map/ppermute | solution.py:414
  9.5 3.0 %collective-permute-start.4 = (f32[8,1024]{1,0:T(8,128)S(1)}, f32[8,1024]{1,0:T(8,128)S(1)}, u32[]{:S(2)}, u32[]{:S(2)}) collective-permute-start(f32[8,1024]{1,0:T(8,128)S(1)} %crossing_rows.1.after), channel_id=1, source_target_pairs={{0,1},{1,0},{2,3},{3,2},{4,5},{5,4},{6,7},{7,6},{8,9},{9,8},{10,11... | collective-permute-start | bytes 98312 | tf_op jit(solution)/shard_map/ppermute | solution.py:366
  14.7 3.4 %collective-permute-start.5 = (bf16[512,1024]{1,0:T(8,128)(2,1)S(1)}, bf16[512,1024]{1,0:T(8,128)(2,1)S(1)}, u32[]{:S(2)}, u32[]{:S(2)}) collective-permute-start(bf16[512,1024]{1,0:T(8,128)(2,1)S(1)} %get-tuple-element.45), channel_id=1, source_target_pairs={{0,1},{1,0},{2,3},{3,2},{4,5},{5,4},{6,7},{7,6},{8,9},{9,8},{10,11... | collective-permute-start | bytes 3145736 | tf_op jit(solution)/shard_map/ppermute | solution.py:366
  15.1 3.0 %copy-start = (f32[1,512,1024]{2,1,0:T(8,128)S(1)}, f32[1,512,1024]{2,1,0:T(8,128)}, u32[]{:S(2)}) copy-start(f32[1,512,1024]{2,1,0:T(8,128)} %param.24) | copy-start | bytes 6291460
  15.1 3.0 %copy-start.1 = (f32[1,512,1024]{2,1,0:T(8,128)S(1)}, f32[1,512,1024]{2,1,0:T(8,128)}, u32[]{:S(2)}) copy-start(f32[1,512,1024]{2,1,0:T(8,128)} %param.19) | copy-start | bytes 6291460
  17.9 3.4 %collective-permute-start.6 = (f32[24,1024]{1,0:T(8,128)S(1)}, f32[24,1024]{1,0:T(8,128)S(1)}, u32[]{:S(2)}, u32[]{:S(2)}) collective-permute-start(f32[24,1024]{1,0:T(8,128)S(1)} %first_gradients.1.refs_1_), channel_id=1, source_target_pairs={{0,1},{1,0},{2,3},{3,2},{4,5},{5,4},{6,7},{7,6},{8,9},{9,8},{10,11... | collective-permute-start | bytes 294920 | tf_op jit(solution)/shard_map/ppermute | solution.py:366
  18.1 3.3 %copy-start.3 = (f32[1,16,1024]{2,1,0:T(8,128)S(1)}, f32[1,16,1024]{2,1,0:T(8,128)}, u32[]{:S(2)}) copy-start(f32[1,16,1024]{2,1,0:T(8,128)} %param.23) | copy-start | bytes 196612
  18.1 3.3 %copy-start.4 = (f32[1,16,1024]{2,1,0:T(8,128)S(1)}, f32[1,16,1024]{2,1,0:T(8,128)}, u32[]{:S(2)}) copy-start(f32[1,16,1024]{2,1,0:T(8,128)} %param.18) | copy-start | bytes 196612
  18.1 3.3 %copy-start.5 = (f32[1,3,1024]{2,0,1:T(1,128)S(1)}, f32[1,3,1024]{2,0,1:T(1,128)}, u32[]{:S(2)}) copy-start(f32[1,3,1024]{2,0,1:T(1,128)} %param.25) | copy-start | bytes 36868
